TPU v7x, 32 devices: a whole 2x2x4 slice. The times are simulated.
32 devices in a mesh: row: 4 (over z), col: 8 (over y, x, core).
Axes of the slice: x: 2, y: 2, z: 4, core: 2. Of those that a mesh axis runs over, the one named last changes fastest.
Arguments:
- page_tokens: bfloat16 [512, 7168], P('row', 'col'), may hold values from -6 to 6
- weight_in: bfloat16 [7168, 28672], P('col', 'row'), may hold values from -0.0625 to 0.0625
- weight_out: bfloat16 [28672, 7168], P('row', 'col'), may hold values from -0.03125 to 0.03125
- upstream: bfloat16 [512, 7168], P('row', 'col'), may hold values from -3 to 3
Outputs:
- block_out: bfloat16 [512, 7168], P('row', 'col')
- grad_tokens: bfloat16 [512, 7168], P('row', 'col')
- grad_weight_in: bfloat16 [7168, 28672], P('col', 'row')
- grad_weight_out: bfloat16 [28672, 7168], P('row', 'col')
All inputs are finite; a program needn't handle non-finite values.
Results may differ from a plain program's by a relative error of at most 0.028.
Values may be sent and summed in bfloat16 or wider, within the bound.
A program may use at most 128 MiB of HBM per device.

v0:
```python
import jax
import jax.numpy as jnp
from jax import lax
from jax.sharding import PartitionSpec as P


def activate(values):
    return (
        0.5
        * values
        * (1.0 + jnp.tanh(0.7978845608 * (values + 0.044715 * values * values * values)))
    )


def activate_back(values, grads):
    return jax.vjp(activate, values)[1](grads)[0]


def contract_last(left, right):
    return lax.dot_general(
        left, right, (((1,), (1,)), ((), ())), preferred_element_type=jnp.float32
    )


def contract_first(left, right):
    return lax.dot_general(
        left, right, (((0,), (0,)), ((), ())), preferred_element_type=jnp.float32
    )


def shards(page_tokens, weight_in, weight_out, upstream):
    features = lax.all_gather(page_tokens, "row", axis=0, tiled=True)
    rows = features
    hidden_pre = lax.psum_scatter(
        jnp.dot(rows, weight_in, preferred_element_type=jnp.float32).astype(jnp.bfloat16),
        "col",
        scatter_dimension=0,
        tiled=True,
    ).astype(jnp.float32)
    active = lax.all_gather(activate(hidden_pre).astype(jnp.bfloat16), "col", axis=0, tiled=True)
    rows = active
    block_out = lax.psum_scatter(
        jnp.dot(rows, weight_out, preferred_element_type=jnp.float32).astype(jnp.bfloat16),
        "row",
        scatter_dimension=0,
        tiled=True,
    )
    upstream_all = lax.all_gather(upstream, "row", axis=0, tiled=True)
    rows = upstream_all
    grad_active = lax.psum_scatter(
        contract_last(rows, weight_out).astype(jnp.bfloat16), "col", scatter_dimension=0, tiled=True
    ).astype(jnp.float32)
    grad_hidden = lax.all_gather(
        activate_back(hidden_pre, grad_active).astype(jnp.bfloat16), "col", axis=0, tiled=True
    )
    rows = grad_hidden
    grad_tokens = lax.psum_scatter(
        contract_last(rows, weight_in).astype(jnp.bfloat16), "row", scatter_dimension=0, tiled=True
    )
    grad_weight_in = contract_first(features, grad_hidden).astype(jnp.bfloat16)
    grad_weight_out = contract_first(active, upstream_all).astype(jnp.bfloat16)
    return (block_out, grad_tokens, grad_weight_in, grad_weight_out)


def solution(mesh):
    placed = (P("row", "col"), P("col", "row"), P("row", "col"), P("row", "col"))
    return jax.shard_map(
        shards,
        mesh=mesh,
        in_specs=placed,
        out_specs=(P("row", "col"), P("row", "col"), P("col", "row"), P("row", "col")),
        check_vma=False,
    )
```

profile of v0, /device:TPU:0, one launch (start us, length us, event | category | flops | bytes accessed | tf_op | source)
XLA Modules:
  0.0 357.3 jit_solution(4376965389833304718)
XLA Ops:
  7.2 0.0 reduce-scatter.9.cloned.1.call-start
  7.2 23.0 %all_gather.14 = bf16[512,896]{1,0:T(8,128)(2,1)S(1)} all-gather(bf16[128,896]{1,0:T(8,128)(2,1)} %param.7), channel_id=1, replica_groups=mesh['row'=4,'col'=8] {'row'}, dimensions={0}, use_global_device_ids=true | all-gather | bytes 1146880 | tf_op jit(solution)/shard_map/all_gather | solution.py:48
  30.2 19.3 %convolution_convert_fusion.1 = bf16[512,7168]{1,0:T(8,128)(2,1)} fusion(bf16[512,896]{1,0:T(8,128)(2,1)S(1)} %all_gather.14, bf16[7168,896]{1,0:T(8,128)(2,1)} %param.6), kind=kOutput, calls=%fused_computation.2 | convolution fusion | flops 6580338688 | bytes 21102592 | tf_op jit(solution)/shard_map/dot_general | solution.py:20
  49.5 0.0 copy-start
  49.5 0.0 reduce-scatter.9.cloned.1.call-update
  49.5 0.0 reduce-scatter.5.cloned.1.call-start
  49.5 0.9 copy-done
  50.4 19.6 %all_gather.12 = bf16[512,896]{1,0:T(8,128)(2,1)S(1)} all-gather(bf16[128,896]{1,0:T(8,128)(2,1)S(1)} %copy-done), channel_id=1, replica_groups=mesh['row'=4,'col'=8] {'row'}, dimensions={0}, use_global_device_ids=true | all-gather | bytes 1146880 | tf_op jit(solution)/shard_map/all_gather | solution.py:32
  70.0 15.4 %convolution_convert_fusion.2 = bf16[512,7168]{1,0:T(8,128)(2,1)} fusion(bf16[512,896]{1,0:T(8,128)(2,1)S(1)} %all_gather.12, bf16[896,7168]{1,0:T(8,128)(2,1)} %param.5), kind=kOutput, calls=%fused_computation.3 | convolution fusion | flops 6580338688 | bytes 21102592 | tf_op jit(solution)/shard_map/dot_general | solution.py:35
  85.4 0.0 reduce-scatter.5.cloned.1.call-update
  85.4 0.0 all-gather.3.cloned.1.call-start
  85.5 30.6 %reduce-scatter.9.cloned.1.call-done = bf16[64,7168]{1,0:T(8,128)(2,1)} async-done(((bf16[512,7168]{1,0:T(8,128)(2,1)}), bf16[64,7168]{1,0:T(8,128)(2,1)}) %reduce-scatter.9.cloned.1.call-update) | async-done | bytes 917520 | tf_op jit(solution)/shard_map/reduce_scatter | solution.py:50
  116.1 71.3 %reduce-scatter.5.cloned.1.call-done = bf16[64,7168]{1,0:T(8,128)(2,1)} async-done(((bf16[512,7168]{1,0:T(8,128)(2,1)}), bf16[64,7168]{1,0:T(8,128)(2,1)}) %reduce-scatter.5.cloned.1.call-update) | async-done | bytes 917520 | tf_op jit(solution)/shard_map/reduce_scatter | solution.py:34
  187.4 4.4 %fusion.7 = (bf16[64,7168]{1,0:T(8,128)(2,1)}, bf16[64,7168]{1,0:T(8,128)(2,1)}) fusion(bf16[64,7168]{1,0:T(8,128)(2,1)} %reduce-scatter.9.cloned.1.call-done, bf16[64,7168]{1,0:T(8,128)(2,1)} %reduce-scatter.5.cloned.1.call-done), kind=kLoop, calls=%fused_computation.21 | loop fusion | flops 12845056 | bytes 3670016 | tf_op jit(solution)/shard_map/convert_element_type | solution.py:54
  191.8 0.0 all-gather.3.cloned.1.call-update
  191.8 0.0 all-gather.5.cloned.1.call-start
  191.8 0.5 all-gather.5.cloned.1.call-update
  192.4 0.0 reduce-scatter.7.cloned.1.call-start
  192.4 49.5 %all-gather.3.cloned.1.call-done = bf16[512,7168]{1,0:T(8,128)(2,1)} async-done(((bf16[64,7168]{1,0:T(8,128)(2,1)}), bf16[512,7168]{1,0:T(8,128)(2,1)}) %all-gather.3.cloned.1.call-update) | async-done | bytes 7340048 | tf_op jit(solution)/shard_map/all_gather | solution.py:40
  241.9 12.9 %convolution_convert_fusion.4 = bf16[512,896]{1,0:T(8,128)(2,1)} fusion(bf16[512,7168]{1,0:T(8,128)(2,1)} %all-gather.3.cloned.1.call-done, bf16[7168,896]{1,0:T(8,128)(2,1)} %param.6), kind=kOutput, calls=%fused_computation.28 | convolution fusion | flops 6577127424 | bytes 21102592 | tf_op jit(solution)/shard_map/dot_general | solution.py:43
  254.8 0.0 reduce-scatter.7.cloned.1.call-update
  254.8 0.2 reduce-scatter.11.cloned.1.call-start
  255.0 39.2 %all-gather.5.cloned.1.call-done = bf16[512,7168]{1,0:T(8,128)(2,1)} async-done(((bf16[64,7168]{1,0:T(8,128)(2,1)}), bf16[512,7168]{1,0:T(8,128)(2,1)}) %all-gather.5.cloned.1.call-update) | async-done | bytes 7340048 | tf_op jit(solution)/shard_map/all_gather | solution.py:53
  294.2 12.9 %convolution_convert_fusion.3 = bf16[512,896]{1,0:T(8,128)(2,1)} fusion(bf16[512,7168]{1,0:T(8,128)(2,1)} %all-gather.5.cloned.1.call-done, bf16[896,7168]{1,0:T(8,128)(2,1)} %param.5), kind=kOutput, calls=%fused_computation.27 | convolution fusion | flops 6577127424 | bytes 21102592 | tf_op jit(solution)/shard_map/dot_general | solution.py:20
  307.1 0.0 reduce-scatter.11.cloned.1.call-update
  307.2 12.9 %convert_bitcast_fusion = bf16[896,7168]{0,1:T(8,128)(2,1)} fusion(bf16[512,7168]{1,0:T(8,128)(2,1)} %all-gather.5.cloned.1.call-done, bf16[512,896]{1,0:T(8,128)(2,1)S(1)} %all_gather.12), kind=kOutput, calls=%fused_computation | convolution fusion | flops 6583091200 | bytes 21102592 | tf_op jit(solution)/shard_map/dot_general | solution.py:26
  320.0 17.6 %copy.8 = bf16[896,7168]{1,0:T(8,128)(2,1)} copy(bf16[896,7168]{0,1:T(8,128)(2,1)} %convert_bitcast_fusion) | data formatting | bytes 25690112
  337.6 12.9 %convolution_convert_fusion = bf16[7168,896]{1,0:T(8,128)(2,1)} fusion(bf16[512,7168]{1,0:T(8,128)(2,1)} %all-gather.3.cloned.1.call-done, bf16[512,896]{1,0:T(8,128)(2,1)S(1)} %all_gather.14), kind=kOutput, calls=%fused_computation.1 | convolution fusion | flops 6583091200 | bytes 21102592 | tf_op jit(solution)/shard_map/dot_general | solution.py:26
  350.4 0.0 reduce-scatter.7.cloned.1.call-done
  350.4 0.0 reduce-scatter.11.cloned.1.call-done
Async XLA Ops:
  7.2 109.0 %reduce-scatter.9.cloned.1.call-start = ((), (), s32[]{:S(2)}) async-start(), calls=%async_computation.7 | async-start | bytes 8257536 | tf_op jit(solution)/shard_map/reduce_scatter | solution.py:50
  49.5 0.9 copy-start
  49.5 137.9 %reduce-scatter.5.cloned.1.call-start = ((), (), s32[]{:S(2)}) async-start(), calls=%async_computation.4 | async-start | bytes 8257536 | tf_op jit(solution)/shard_map/reduce_scatter | solution.py:34
  85.4 156.5 %all-gather.3.cloned.1.call-start = ((), (), s32[]{:S(2)}) async-start(), calls=%async_computation.5 | async-start | bytes 8257536 | tf_op jit(solution)/shard_map/all_gather | solution.py:40
  191.8 102.4 %all-gather.5.cloned.1.call-start = ((), (), s32[]{:S(2)}) async-start(), calls=%async_computation.8 | async-start | bytes 8257536 | tf_op jit(solution)/shard_map/all_gather | solution.py:53
  192.4 158.1 %reduce-scatter.7.cloned.1.call-start = ((), (), s32[]{:S(2)}) async-start(), calls=%async_computation.6 | async-start | bytes 1146880 | tf_op jit(solution)/shard_map/reduce_scatter | solution.py:42
  254.8 95.6 %reduce-scatter.11.cloned.1.call-start = ((), (), s32[]{:S(2)}) async-start(), calls=%async_computation.9 | async-start | bytes 1146880 | tf_op jit(solution)/shard_map/reduce_scatter | solution.py:57
Sparse Core Ops, SparseCore 0:
  49.6 66.4 reduce-scatter.8
  120.5 66.9 reduce-scatter.4
  191.9 49.9 all-gather.2
  244.2 49.9 all-gather.4
  296.9 25.0 reduce-scatter.6
  324.8 24.0 reduce-scatter.10
where the time goes:
time: 358 us; the launch traced here: 357 us
  waiting for transfers between devices  191 us (53%)
  matrix products  86.2 us (24%)
  blocking collectives  42.6 us (12%)
  local copies, waits for them, and re-layouts  18.4 us (5%)
  between operations  14.1 us (4%)
  other arithmetic  4.36 us (1%)
    reduce_scatter x1, waiting for transfers between devices, shards(): lax.psum_scatter(jnp.dot(rows, weight_in, preferred_element_type=jnp.floa...  71.3 us
    all_gather x1, waiting for transfers between devices, shards(): lax.all_gather(activate(hidden_pre).astype(jnp.bfloat16), 'col', axis=0,...  49.5 us
    all_gather x1, waiting for transfers between devices, shards(): lax.all_gather(activate_back(hidden_pre, grad_active).astype(jnp.bfloat16...  39.2 us
    dot_general x2, matrix products, contract_last(): lax.dot_general(left, right, (((1,), (1,)), ((), ())), preferred_element_...  32.2 us
    reduce_scatter x1, waiting for transfers between devices, shards(): lax.psum_scatter(contract_last(rows, weight_out).astype(jnp.bfloat16), 'c...  30.6 us
    dot_general x2, matrix products, contract_first(): lax.dot_general(left, right, (((0,), (0,)), ((), ())), preferred_element_...  25.7 us
    all_gather x1, blocking collectives, shards(): upstream_all = lax.all_gather(upstream, 'row', axis=0, tiled=True)  23 us
    all_gather x1, blocking collectives, shards(): features = lax.all_gather(page_tokens, 'row', axis=0, tiled=True)  19.6 us
  transfers between devices with their start and end apart: 6, of which 4 were waited for; matrix products, arithmetic and copies ran while one was open for 24% of the time, Pallas kernels for 0%

commit v1 on v0

v1 whole, which is shorter than its diff:
```python
import functools

import jax
import jax.numpy as jnp
from jax import lax
from jax.experimental import pallas as pl
from jax.experimental.pallas import tpu as pltpu
from jax.sharding import PartitionSpec as P

MESH = pl.DeviceIdType.MESH
RING = 8
BF = jnp.bfloat16
F32 = jnp.float32


def activate(values):
    return (
        0.5
        * values
        * (1.0 + jnp.tanh(0.7978845608 * (values + 0.044715 * values * values * values)))
    )


def slope(values):
    square = values * values
    bend = jnp.tanh(0.7978845608 * (values + 0.044715 * square * values))
    return 0.5 * (1.0 + bend) + 0.5 * values * (1.0 - bend * bend) * (
        0.7978845608 * (1.0 + 0.134145 * square)
    )


def contract_last(left, right):
    return lax.dot_general(left, right, (((1,), (1,)), ((), ())), preferred_element_type=F32)


def contract_first(left, right):
    return lax.dot_general(left, right, (((0,), (0,)), ((), ())), preferred_element_type=F32)


def kernel(
    n_row,
    n_col,
    tokens_ref,
    upstream_ref,
    weight_in,
    weight_out,
    block_part,
    token_part,
    active_out,
    hidden_out,
    features_out,
    upstream_out,
    *scratch,
):
    levels = n_col.bit_length() - 1
    piles = scratch[: levels]
    landed = scratch[levels : 2 * levels]
    (
        gathered,
        held_in,
        held_out,
        features,
        upstream,
        pre,
        total,
        stage_send,
        stage_recv,
        spread_send,
        spread_recv,
        row_send,
        row_recv,
        weight_sem,
        out_sem,
        side_sem,
    ) = scratch[2 * levels :]
    chunks, depth, width = held_in.shape
    tall = features.shape[0]
    rows = tokens_ref.shape[0]
    steps = 2 * chunks
    here = lax.axis_index("row")
    me = lax.axis_index("col")

    bits = [(me // 2**j) % 2 for j in range(levels)]
    strides = [2**j for j in range(levels)]
    if levels == 3:
        core, bx, by = bits
        bits = [core, bx * (1 - core) + by * core, by * (1 - core) + bx * core]
        strides = [1, 2 + 2 * core, 4 - 2 * core]
    mates = [me + s * (1 - 2 * b) for s, b in zip(strides, bits)]
    sizes = [tall >> (j + 1) for j in range(levels)]
    starts = [0]
    for j in range(levels):
        starts.append(starts[-1] + bits[j] * sizes[j])

    barrier = pltpu.get_barrier_semaphore()
    for mate in mates:
        pl.semaphore_signal(barrier, inc=1, device_id=(here, mate), device_id_type=MESH)

    @pl.when(here > 0)
    def _():
        pl.semaphore_signal(barrier, inc=1, device_id=(here - 1, me), device_id_type=MESH)

    @pl.when(here < n_row - 1)
    def _():
        pl.semaphore_signal(barrier, inc=1, device_id=(here + 1, me), device_id_type=MESH)

    def load_in(k):
        return pltpu.make_async_copy(
            weight_in.at[:, pl.ds(pl.multiple_of(k * width, width), width)],
            held_in.at[k],
            weight_sem.at[0, k],
        )

    def load_out(k):
        return pltpu.make_async_copy(
            weight_out.at[pl.ds(pl.multiple_of(k * width, width), width), :],
            held_out.at[k],
            weight_sem.at[1, k],
        )

    @pl.loop(0, chunks)
    def _(k):
        load_in(k).start()

    sources = (tokens_ref, upstream_ref)
    whole = (features, upstream)

    def block_of(kind, origin):
        return whole[kind].at[pl.ds(pl.multiple_of(origin * rows, rows), rows), :]

    def hop(kind, way, dist):
        origin = here - dist if way == 0 else here + dist
        goal = here + 1 if way == 0 else here - 1
        source = sources[kind] if dist == 0 else block_of(kind, origin)
        return pltpu.make_async_remote_copy(
            src_ref=source,
            dst_ref=block_of(kind, origin),
            send_sem=row_send.at[kind, way, dist],
            recv_sem=row_recv.at[kind, way, dist],
            device_id=(goal, me),
            device_id_type=MESH,
        )

    def sends(way, dist):
        if way == 0:
            return (here >= dist) & (here < n_row - 1)
        return (here < n_row - dist) & (here > 0)

    def takes(way, dist):
        return here >= dist + 1 if way == 0 else here < n_row - dist - 1

    def arrive(kind, dist):
        for way in (0, 1):

            @pl.when(takes(way, dist))
            def _(way=way):
                origin = here - dist - 1 if way == 0 else here + dist + 1
                pltpu.make_async_remote_copy(
                    src_ref=block_of(kind, origin),
                    dst_ref=block_of(kind, origin),
                    send_sem=row_send.at[kind, way, dist],
                    recv_sem=row_recv.at[kind, way, dist],
                    device_id=(here - 1 if way == 0 else here + 1, me),
                    device_id_type=MESH,
                ).wait_recv()

            if dist + 1 < n_row - 1:

                @pl.when(sends(way, dist + 1))
                def _(way=way):
                    hop(kind, way, dist + 1).start()

    neighbours = jnp.where(here > 0, 1, 0) + jnp.where(here < n_row - 1, 1, 0)
    pl.semaphore_wait(barrier, levels + neighbours)

    for kind in (0, 1):
        for way in (0, 1):

            @pl.when(sends(way, 0))
            def _(kind=kind, way=way):
                hop(kind, way, 0).start()

    @pl.loop(0, chunks)
    def _(k):
        load_out(k).start()

    own = pl.ds(pl.multiple_of(here * rows, rows), rows)
    features[own, :] = tokens_ref[...]
    upstream[own, :] = upstream_ref[...]
    for dist in range(n_row - 1):
        arrive(0, dist)
    pltpu.make_async_copy(features, features_out, side_sem.at[0]).start()

    def stage(j, t):
        other = pl.multiple_of((1 - bits[j]) * sizes[j], sizes[j])
        return pltpu.make_async_remote_copy(
            src_ref=piles[j].at[lax.rem(t, 2), pl.ds(other, sizes[j]), :],
            dst_ref=landed[j].at[lax.rem(t, RING)],
            send_sem=stage_send.at[j, lax.rem(t, 2)],
            recv_sem=stage_recv.at[j, lax.rem(t, RING)],
            device_id=(here, mates[j]),
            device_id_type=MESH,
        )

    def spread(j, t, mine=True):
        at = starts[j + 1] if mine else starts[j] + (1 - bits[j]) * sizes[j]
        view = gathered.at[lax.rem(t, RING), pl.ds(pl.multiple_of(at, sizes[j]), sizes[j]), :]
        return pltpu.make_async_remote_copy(
            src_ref=view,
            dst_ref=view,
            send_sem=spread_send.at[j, lax.rem(t, 2)],
            recv_sem=spread_recv.at[j, lax.rem(t, RING)],
            device_id=(here, mates[j]),
            device_id_type=MESH,
        )

    def columns(k):
        return pl.ds(pl.multiple_of(k * width, width), width)

    def put_active(t):
        return pltpu.make_async_copy(
            gathered.at[lax.rem(t, RING)], active_out.at[:, columns(t)], out_sem.at[lax.rem(t, 2)]
        )

    def put_hidden(t):
        return pltpu.make_async_copy(
            gathered.at[lax.rem(t, RING)],
            hidden_out.at[:, columns(t - chunks)],
            out_sem.at[lax.rem(t, 2)],
        )

    tile = min(256, tall)

    def during(t, act):
        pl.when((t >= 0) & (t < steps))(act)

    def produce(t):
        slot = lax.rem(t, 2)

        @pl.when(t < chunks)
        def _():
            load_in(t).wait()

            @pl.loop(0, tall // tile)
            def _(r):
                at = pl.ds(pl.multiple_of(r * tile, tile), tile)
                piles[0][slot, at, :] = jnp.dot(
                    features[at, :], held_in[t], preferred_element_type=F32
                ).astype(BF)

        @pl.when(t >= chunks)
        def _():
            @pl.loop(0, tall // tile)
            def _(r):
                at = pl.ds(pl.multiple_of(r * tile, tile), tile)
                piles[0][slot, at, :] = contract_last(
                    upstream[at, :], held_out[t - chunks]
                ).astype(BF)

        stage(0, t).start()

    def fold(j, t):
        copy = stage(j, t)
        copy.wait_send()
        copy.wait_recv()
        slot, ring = lax.rem(t, 2), lax.rem(t, RING)
        part = min(32, sizes[j])
        keep = bits[j] * sizes[j]

        if j < levels - 1:
            def combine(r):
                at = pl.ds(pl.multiple_of(r * part, part), part)
                held = pl.ds(pl.multiple_of(keep + r * part, part), part)
                piles[j + 1][slot, at, :] = (
                    piles[j][slot, held, :].astype(F32) + landed[j][ring, at, :].astype(F32)
                ).astype(BF)

            count = sizes[j + 1] // part
            other = (1 - bits[j + 1]) * count

            @pl.loop(0, count)
            def _(r):
                combine(other + r)

            stage(j + 1, t).start()
            mine = bits[j + 1] * count

            @pl.loop(0, count)
            def _(r):
                combine(mine + r)
        else:
            k = lax.rem(t, chunks)

            @pl.loop(0, sizes[j] // part)
            def _(r):
                at = pl.ds(pl.multiple_of(r * part, part), part)
                held = pl.ds(pl.multiple_of(keep + r * part, part), part)
                target = pl.ds(pl.multiple_of(starts[levels] + r * part, part), part)
                value = piles[j][slot, held, :].astype(F32) + landed[j][ring, at, :].astype(F32)

                @pl.when(t < chunks)
                def _():
                    pre[k, at, :] = value
                    gathered[ring, target, :] = activate(value).astype(BF)

                @pl.when(t >= chunks)
                def _():
                    gathered[ring, target, :] = (value * slope(pre[k, at, :])).astype(BF)

            spread(j, t).start()

    def gather(j, t):
        spread(j, t).wait_send()
        spread(j, t, mine=False).wait_recv()
        spread(j - 1, t).start()

    def consume(t):
        spread(0, t).wait_send()
        spread(0, t, mine=False).wait_recv()
        ring = lax.rem(t, RING)
        k = lax.rem(t, chunks)

        @pl.when(k == 0)
        def _():
            total[...] = jnp.zeros_like(total)

        @pl.when(t < chunks)
        def _():
            put_active(t).start()
            load_out(t).wait()

            @pl.loop(0, tall // tile)
            def _(r):
                at = pl.ds(pl.multiple_of(r * tile, tile), tile)
                total[at, :] += jnp.dot(
                    gathered[ring, at, :], held_out[t], preferred_element_type=F32
                )

        @pl.when(t >= chunks)
        def _():
            put_hidden(t).start()

            @pl.loop(0, tall // tile)
            def _(r):
                at = pl.ds(pl.multiple_of(r * tile, tile), tile)
                total[at, :] += contract_last(gathered[ring, at, :], held_in[t - chunks])

        @pl.when(t == chunks - 1)
        def _():
            block_part[...] = total[...].astype(BF)

        @pl.when(t == steps - 1)
        def _():
            token_part[...] = total[...].astype(BF)

    def written(t):
        @pl.when(t < chunks)
        def _():
            put_active(t).wait()

        @pl.when(t >= chunks)
        def _():
            put_hidden(t).wait()

    lag = 2 * levels

    @pl.loop(0, steps + lag + 1)
    def _(i):
        during(i - lag - 1, lambda: written(i - lag - 1))
        during(i - lag, lambda: consume(i - lag))
        for j in range(1, levels):
            t = i - lag + j
            during(t, functools.partial(gather, j, t))
        for j in range(levels - 1, -1, -1):
            t = i - j - 1
            during(t, functools.partial(fold, j, t))
        during(i, lambda: produce(i))
        for dist in range(n_row - 1):

            @pl.when(i == dist)
            def _(dist=dist):
                arrive(1, dist)

    side = pltpu.make_async_copy(upstream, upstream_out, side_sem.at[1])
    side.start()
    side.wait()
    pltpu.make_async_copy(features, features_out, side_sem.at[0]).wait()
    for kind in (0, 1):
        for dist in range(n_row - 1):
            for way in (0, 1):

                @pl.when(sends(way, dist))
                def _(kind=kind, way=way, dist=dist):
                    hop(kind, way, dist).wait_send()


def encode(n_row, n_col, page_tokens, upstream, weight_in, weight_out):
    rows, depth = page_tokens.shape
    hidden = weight_in.shape[1]
    tall = rows * n_row
    levels = n_col.bit_length() - 1
    chunks = 14
    width = hidden // chunks
    vmem = pl.BlockSpec(memory_space=pltpu.VMEM)
    anywhere = pl.BlockSpec(memory_space=pl.ANY)
    dma = pltpu.SemaphoreType.DMA
    shape = jax.ShapeDtypeStruct
    flops = 8 * tall * depth * hidden
    return pl.pallas_call(
        functools.partial(kernel, n_row, n_col),
        out_shape=[
            shape((tall, depth), BF),
            shape((tall, depth), BF),
            shape((tall, hidden), BF),
            shape((tall, hidden), BF),
            shape((tall, depth), BF),
            shape((tall, depth), BF),
        ],
        in_specs=[vmem, vmem, anywhere, anywhere],
        out_specs=[vmem, vmem, anywhere, anywhere, anywhere, anywhere],
        scratch_shapes=[pltpu.VMEM((2, tall >> j, width), BF) for j in range(levels)]
        + [pltpu.VMEM((RING, tall >> (j + 1), width), BF) for j in range(levels)]
        + [
            pltpu.VMEM((RING, tall, width), BF),
            pltpu.VMEM((chunks, depth, width), BF),
            pltpu.VMEM((chunks, width, depth), BF),
            pltpu.VMEM((tall, depth), BF),
            pltpu.VMEM((tall, depth), BF),
            pltpu.VMEM((chunks, tall >> levels, width), F32),
            pltpu.VMEM((tall, depth), F32),
            dma((levels, 2)),
            dma((levels, RING)),
            dma((levels, 2)),
            dma((levels, RING)),
            dma((2, 2, n_row)),
            dma((2, 2, n_row)),
            dma((2, chunks)),
            dma((2,)),
            dma((2,)),
        ],
        compiler_params=pltpu.CompilerParams(
            collective_id=0, has_side_effects=True, vmem_limit_bytes=58 * 2**20
        ),
        cost_estimate=pl.CostEstimate(
            flops=flops, bytes_accessed=8 * depth * hidden, transcendentals=0
        ),
    )(page_tokens, upstream, weight_in, weight_out)


def shards(n_row, n_col, page_tokens, weight_in, weight_out, upstream):
    block_part, token_part, active, grad_hidden, features, upstream_all = encode(
        n_row, n_col, page_tokens, upstream, weight_in, weight_out
    )
    block_out = lax.psum_scatter(block_part, "row", scatter_dimension=0, tiled=True)
    grad_tokens = lax.psum_scatter(token_part, "row", scatter_dimension=0, tiled=True)
    grad_weight_in = contract_first(features, grad_hidden).astype(BF)
    grad_weight_out = contract_first(active, upstream_all).astype(BF)
    return (block_out, grad_tokens, grad_weight_in, grad_weight_out)


def solution(mesh):
    placed = (P("row", "col"), P("col", "row"), P("row", "col"), P("row", "col"))
    return jax.shard_map(
        functools.partial(shards, mesh.shape["row"], mesh.shape["col"]),
        mesh=mesh,
        in_specs=placed,
        out_specs=(P("row", "col"), P("row", "col"), P("col", "row"), P("row", "col")),
        check_vma=False,
    )
```

time: 358 us -> 255 us (0.71)
  Pallas kernels: 0 us -> 191 us
  waiting for transfers between devices: 191 us -> 26.6 us
  matrix products: 86.2 us -> 23.3 us
  blocking collectives: 42.6 us -> 0 us
  local copies, waits for them, and re-layouts: 18.4 us -> 0.01 us
  other arithmetic: 4.36 us -> 0.01 us
    pallas_call x0 -> x1, Pallas kernels: none -> 191 us  [encode(): pl.pallas_call(functools.partial(kernel, n_row, n_col), out_shape=[shape(...]
    all_gather x2 -> x0, waiting for transfers between devices: 88.6 us -> none  [the longest x1 49.5 us: shards(): lax.all_gather(activate(hidden_pre).astype(jnp.bfloat16), 'col', axis=0,...]
    reduce_scatter x4 -> x2, waiting for transfers between devices: 102 us -> 25.9 us  [the longest x1 25.9 us: shards(): lax.psum_scatter(token_part, 'row', scatter_dimension=0, tiled=True)]
    dot_general x4 -> x0, matrix products: 60.5 us -> none  [the longest x2 32.2 us: contract_last(): lax.dot_general(left, right, (((1,), (1,)), ((), ())), preferred_element_...]
    all_gather x2 -> x0, blocking collectives: 42.6 us -> none  [the longest x1 23 us: shards(): upstream_all = lax.all_gather(upstream, 'row', axis=0, tiled=True)]
    unnamed x3 -> x6, local copies, waits for them, and re-layouts: 18.4 us -> 0.01 us
    convert_element_type x1 -> x0, other arithmetic: 4.36 us -> none  [shards(): activate_back(hidden_pre, grad_active).astype(jnp.bfloat16)]
  transfers between devices with their start and end apart: 6 -> 2, of which waited for: 4 -> 1; matrix products, arithmetic and copies ran while one was open for 24% -> 9% of each run, Pallas kernels for 0% -> 0%
where the time goes in v1:
time: 255 us
  Pallas kernels  191 us (75%)
  waiting for transfers between devices  26.6 us (10%)
  matrix products  23.3 us (9%)
  between operations  14.1 us (6%)
    pallas_call x1, Pallas kernels, encode(): pl.pallas_call(functools.partial(kernel, n_row, n_col), out_shape=[shape(...  191 us
    reduce_scatter x1, waiting for transfers between devices, shards(): lax.psum_scatter(token_part, 'row', scatter_dimension=0, tiled=True)  25.9 us
    dot_general x2, matrix products, contract_first(): lax.dot_general(left, right, (((0,), (0,)), ((), ())), preferred_element_...  23.3 us
  transfers between devices with their start and end apart: 2, of which 1 were waited for; matrix products, arithmetic and copies ran while one was open for 9% of the time, Pallas kernels for 0%

profile of v1, /device:TPU:0, one launch (start us, length us, event | category | flops | bytes accessed | tf_op | source)
XLA Modules:
  0.0 254.9 jit_solution(14960788263852136901)
XLA Ops:
  7.2 0.0 reduce-scatter.3.cloned.1.call-start
  7.2 190.9 %shard_map.75 = (bf16[512,896]{1,0:T(8,128)(2,1)}, bf16[512,896]{1,0:T(8,128)(2,1)}, bf16[512,7168]{1,0:T(8,128)(2,1)}, bf16[512,7168]{1,0:T(8,128)(2,1)}, bf16[...) custom-call(bf16[128,896]{1,0:T(8,128)(2,1)} %tokens_ref.1, bf16[128,896]{1,0:T(8,128)(2,1)} %upstream_ref.1, ...), custom_call_target="tpu_custom_call" | custom-call | flops 26306674688 | bytes 51380224 | tf_op jit(solution)/shard_map/pallas_call | solution.py:409
  198.1 0.0 reduce-scatter.3.cloned.1.call-update
  198.1 0.0 reduce-scatter.5.cloned.1.call-start
  198.1 0.0 slice-start
  198.2 0.7 reduce-scatter.5.cloned.1.call-update
  198.9 0.0 slice-start.1
  198.9 0.0 copy-start
  198.9 13.3 %convolution_convert_fusion = bf16[7168,896]{1,0:T(8,128)(2,1)} fusion(bf16[512,7168]{1,0:T(8,128)(2,1)} %get-tuple-element.14, bf16[512,896]{1,0:T(8,128)(2,1)} %get-tuple-element.15), kind=kOutput, calls=%fused_computation | convolution fusion | flops 6583091200 | bytes 21102592 | tf_op jit(solution)/shard_map/dot_general | solution.py:37
  212.2 0.0 slice-done
  212.2 0.0 slice-done.1
  212.2 0.0 copy-done
  212.2 9.9 %convolution_convert_fusion.1 = bf16[896,7168]{1,0:T(8,128)(2,1)} fusion(bf16[512,896]{1,0:T(8,128)(2,1)S(1)} %copy-done, bf16[512,7168]{1,0:T(8,128)(2,1)S(1)} %bitcast.5), kind=kOutput, calls=%fused_computation.1 | convolution fusion | flops 6583091200 | bytes 21102592 | tf_op jit(solution)/shard_map/dot_general | solution.py:37
  222.2 0.0 reduce-scatter.3.cloned.1.call-done
  222.2 25.9 %reduce-scatter.5.cloned.1.call-done = bf16[128,896]{1,0:T(8,128)(2,1)} async-done(((bf16[512,896]{1,0:T(8,128)(2,1)}), bf16[128,896]{1,0:T(8,128)(2,1)}) %reduce-scatter.5.cloned.1.call-update) | async-done | bytes 229392 | tf_op jit(solution)/shard_map/reduce_scatter | solution.py:455
  (1 shorter events, 0.0 us)
Async XLA Ops:
  7.2 215.0 %reduce-scatter.3.cloned.1.call-start = ((), (), s32[]{:S(2)}) async-start(), calls=%async_computation.2 | async-start | bytes 1146880 | tf_op jit(solution)/shard_map/reduce_scatter | solution.py:454
  198.1 50.0 %reduce-scatter.5.cloned.1.call-start = ((), (), s32[]{:S(2)}) async-start(), calls=%async_computation.3 | async-start | bytes 1146880 | tf_op jit(solution)/shard_map/reduce_scatter | solution.py:455
  198.1 14.1 %slice-start = ((s8[7340032]{0:T(1024)(128)(4,1)}), s8[3145728]{0:T(1024)(128)(4,1)S(1)}, s32[]{:S(2)}) async-start(s8[7340032]{0:T(1024)(128)(4,1)} %bitcast.4), calls=%async_computation.4 | async-start | bytes 6291456
  198.9 13.4 %slice-start.1 = ((s8[7340032]{0:T(1024)(128)(4,1)}), s8[4194304]{0:T(1024)(128)(4,1)S(1)}, s32[]{:S(2)}) async-start(s8[7340032]{0:T(1024)(128)(4,1)} %bitcast.4), calls=%async_computation.5 | async-start | bytes 8388608
  198.9 13.4 %copy-start = (bf16[512,896]{1,0:T(8,128)(2,1)S(1)}, bf16[512,896]{1,0:T(8,128)(2,1)}, u32[]{:S(2)}) copy-start(bf16[512,896]{1,0:T(8,128)(2,1)} %get-tuple-element.12) | copy-start | bytes 2752516
Sparse Core Ops, SparseCore 0:
  198.2 22.8 reduce-scatter.2
  224.0 24.0 reduce-scatter.4

commit v2 on v1

--- a/solution.py
+++ b/solution.py
@@ -8,7 +8,7 @@
 from jax.sharding import PartitionSpec as P
 
 MESH = pl.DeviceIdType.MESH
-RING = 8
+RING = 12
 BF = jnp.bfloat16
 F32 = jnp.float32
 
@@ -44,7 +44,7 @@
     upstream_ref,
     weight_in,
     weight_out,
-    block_part,
+    block_out,
     token_part,
     active_out,
     hidden_out,
@@ -72,6 +72,10 @@
         weight_sem,
         out_sem,
         side_sem,
+        block_part,
+        block_landed,
+        block_send,
+        block_recv,
     ) = scratch[2 * levels :]
     chunks, depth, width = held_in.shape
     tall = features.shape[0]
@@ -96,13 +100,10 @@
     for mate in mates:
         pl.semaphore_signal(barrier, inc=1, device_id=(here, mate), device_id_type=MESH)
 
-    @pl.when(here > 0)
-    def _():
-        pl.semaphore_signal(barrier, inc=1, device_id=(here - 1, me), device_id_type=MESH)
-
-    @pl.when(here < n_row - 1)
-    def _():
-        pl.semaphore_signal(barrier, inc=1, device_id=(here + 1, me), device_id_type=MESH)
+    for d in range(1, n_row):
+        pl.semaphore_signal(
+            barrier, inc=1, device_id=(lax.rem(here + d, n_row), me), device_id_type=MESH
+        )
 
     def load_in(k):
         return pltpu.make_async_copy(
@@ -170,15 +171,27 @@
                 def _(way=way):
                     hop(kind, way, dist + 1).start()
 
-    neighbours = jnp.where(here > 0, 1, 0) + jnp.where(here < n_row - 1, 1, 0)
-    pl.semaphore_wait(barrier, levels + neighbours)
-
-    for kind in (0, 1):
+    pl.semaphore_wait(barrier, levels + n_row - 1)
+
+    def open_rows(kind):
         for way in (0, 1):
 
             @pl.when(sends(way, 0))
-            def _(kind=kind, way=way):
+            def _(way=way):
                 hop(kind, way, 0).start()
+
+    def hand_over(d):
+        goal = lax.rem(here + d, n_row)
+        return pltpu.make_async_remote_copy(
+            src_ref=block_part.at[pl.ds(pl.multiple_of(goal * rows, rows), rows), :],
+            dst_ref=block_landed.at[d - 1],
+            send_sem=block_send.at[d - 1],
+            recv_sem=block_recv.at[d - 1],
+            device_id=(goal, me),
+            device_id_type=MESH,
+        )
+
+    open_rows(0)
 
     @pl.loop(0, chunks)
     def _(k):
@@ -189,6 +202,7 @@
     upstream[own, :] = upstream_ref[...]
     for dist in range(n_row - 1):
         arrive(0, dist)
+    open_rows(1)
     pltpu.make_async_copy(features, features_out, side_sem.at[0]).start()
 
     def stage(j, t):
@@ -229,7 +243,7 @@
             out_sem.at[lax.rem(t, 2)],
         )
 
-    tile = min(256, tall)
+    tile = min(512, tall)
 
     def during(t, act):
         pl.when((t >= 0) & (t < steps))(act)
@@ -348,6 +362,8 @@
         @pl.when(t == chunks - 1)
         def _():
             block_part[...] = total[...].astype(BF)
+            for d in range(1, n_row):
+                hand_over(d).start()
 
         @pl.when(t == steps - 1)
         def _():
@@ -362,27 +378,41 @@
         def _():
             put_hidden(t).wait()
 
-    lag = 2 * levels
+    folds = [1 + 2 * j for j in range(levels)]
+    gathers = [folds[-1] + 2 * (levels - j) for j in range(levels)]
+    lag = gathers[1] + 1
+    pace = max(1, (chunks - 1) // n_row)
 
     @pl.loop(0, steps + lag + 1)
     def _(i):
         during(i - lag - 1, lambda: written(i - lag - 1))
         during(i - lag, lambda: consume(i - lag))
         for j in range(1, levels):
-            t = i - lag + j
-            during(t, functools.partial(gather, j, t))
+            during(i - gathers[j], functools.partial(gather, j, i - gathers[j]))
         for j in range(levels - 1, -1, -1):
-            t = i - j - 1
-            during(t, functools.partial(fold, j, t))
+            during(i - folds[j], functools.partial(fold, j, i - folds[j]))
         during(i, lambda: produce(i))
         for dist in range(n_row - 1):
 
-            @pl.when(i == dist)
+            @pl.when(i == pace * (dist + 1))
             def _(dist=dist):
                 arrive(1, dist)
 
     side = pltpu.make_async_copy(upstream, upstream_out, side_sem.at[1])
     side.start()
+    part = min(32, rows)
+    for d in range(1, n_row):
+        hand_over(d).wait()
+
+    @pl.loop(0, rows // part)
+    def _(r):
+        at = pl.ds(pl.multiple_of(r * part, part), part)
+        held = pl.ds(pl.multiple_of(here * rows + r * part, part), part)
+        value = block_part[held, :].astype(F32)
+        for d in range(1, n_row):
+            value += block_landed[d - 1, at, :].astype(F32)
+        block_out[at, :] = value.astype(BF)
+
     side.wait()
     pltpu.make_async_copy(features, features_out, side_sem.at[0]).wait()
     for kind in (0, 1):
@@ -409,7 +439,7 @@
     return pl.pallas_call(
         functools.partial(kernel, n_row, n_col),
         out_shape=[
-            shape((tall, depth), BF),
+            shape((rows, depth), BF),
             shape((tall, depth), BF),
             shape((tall, hidden), BF),
             shape((tall, hidden), BF),
@@ -437,6 +467,10 @@
             dma((2, chunks)),
             dma((2,)),
             dma((2,)),
+            pltpu.VMEM((tall, depth), BF),
+            pltpu.VMEM((n_row - 1, rows, depth), BF),
+            dma((n_row - 1,)),
+            dma((n_row - 1,)),
         ],
         compiler_params=pltpu.CompilerParams(
             collective_id=0, has_side_effects=True, vmem_limit_bytes=58 * 2**20
@@ -448,10 +482,9 @@
 
 
 def shards(n_row, n_col, page_tokens, weight_in, weight_out, upstream):
-    block_part, token_part, active, grad_hidden, features, upstream_all = encode(
+    block_out, token_part, active, grad_hidden, features, upstream_all = encode(
         n_row, n_col, page_tokens, upstream, weight_in, weight_out
     )
-    block_out = lax.psum_scatter(block_part, "row", scatter_dimension=0, tiled=True)
     grad_tokens = lax.psum_scatter(token_part, "row", scatter_dimension=0, tiled=True)
     grad_weight_in = contract_first(features, grad_hidden).astype(BF)
     grad_weight_out = contract_first(active, upstream_all).astype(BF)

time: 255 us -> 196 us (0.77)
  Pallas kernels: 191 us -> 157 us
  waiting for transfers between devices: 26.6 us -> 1.66 us
    pallas_call x1, Pallas kernels: 191 us -> 157 us  [encode(): pl.pallas_call(functools.partial(kernel, n_row, n_col), out_shape=[shape(...]
    reduce_scatter x1, waiting for transfers between devices: 25.9 us -> 1.64 us  [shards(): lax.psum_scatter(token_part, 'row', scatter_dimension=0, tiled=True)]
  transfers between devices with their start and end apart: 2 -> 1, of which waited for: 1 -> 1; matrix products, arithmetic and copies ran while one was open for 9% -> 12% of each run, Pallas kernels for 0% -> 0%
where the time goes in v2:
time: 196 us
  Pallas kernels  157 us (80%)
  matrix products  23.2 us (12%)
  between operations  14.1 us (7%)
    pallas_call x1, Pallas kernels, encode(): pl.pallas_call(functools.partial(kernel, n_row, n_col), out_shape=[shape(...  157 us
    dot_general x2, matrix products, contract_first(): lax.dot_general(left, right, (((0,), (0,)), ((), ())), preferred_element_...  23.2 us
  transfers between devices with their start and end apart: 1, of which 1 were waited for; matrix products, arithmetic and copies ran while one was open for 12% of the time, Pallas kernels for 0%

profile of v2, /device:TPU:0, one launch (start us, length us, event | category | flops | bytes accessed | tf_op | source)
XLA Modules:
  0.0 196.3 jit_solution(16850019554538611198)
XLA Ops:
  7.2 0.0 reduce-scatter.2.cloned.1.call-start
  7.2 156.6 %shard_map.75 = (bf16[128,896]{1,0:T(8,128)(2,1)}, bf16[512,896]{1,0:T(8,128)(2,1)}, bf16[512,7168]{1,0:T(8,128)(2,1)}, bf16[512,7168]{1,0:T(8,128)(2,1)}, bf16[...) custom-call(bf16[128,896]{1,0:T(8,128)(2,1)} %tokens_ref.1, bf16[128,896]{1,0:T(8,128)(2,1)} %upstream_ref.1, ...), custom_call_target="tpu_custom_call" | custom-call | flops 26306674688 | bytes 51380224 | tf_op jit(solution)/shard_map/pallas_call | solution.py:439
  163.9 0.0 reduce-scatter.2.cloned.1.call-update
  163.9 0.0 copy-start.1
  163.9 0.0 copy-start.2
  163.9 13.2 %convolution_convert_fusion = bf16[7168,896]{1,0:T(8,128)(2,1)} fusion(bf16[512,7168]{1,0:T(8,128)(2,1)} %get-tuple-element.14, bf16[512,896]{1,0:T(8,128)(2,1)} %get-tuple-element.15), kind=kOutput, calls=%fused_computation | convolution fusion | flops 6583091200 | bytes 21102592 | tf_op jit(solution)/shard_map/dot_general | solution.py:37
  177.2 0.0 copy-start
  177.2 0.0 copy-done.1
  177.2 0.0 copy-done.2
  177.2 9.9 %convolution_convert_fusion.1 = bf16[896,7168]{1,0:T(8,128)(2,1)} fusion(bf16[512,896]{1,0:T(8,128)(2,1)S(1)} %copy-done.2, bf16[512,7168]{1,0:T(8,128)(2,1)S(1)} %copy-done.1), kind=kOutput, calls=%fused_computation.1 | convolution fusion | flops 6583091200 | bytes 21102592 | tf_op jit(solution)/shard_map/dot_general | solution.py:37
  187.1 1.6 reduce-scatter.2.cloned.1.call-done
  188.7 0.0 copy-done
  188.7 0.7 copy.9
Async XLA Ops:
  7.2 181.6 %reduce-scatter.2.cloned.1.call-start = ((), (), s32[]{:S(2)}) async-start(), calls=%async_computation.1 | async-start | bytes 1146880 | tf_op jit(solution)/shard_map/reduce_scatter | solution.py:488
  163.9 13.3 %copy-start.1 = (bf16[512,7168]{1,0:T(8,128)(2,1)S(1)}, bf16[512,7168]{1,0:T(8,128)(2,1)}, u32[]{:S(2)}) copy-start(bf16[512,7168]{1,0:T(8,128)(2,1)} %get-tuple-element.13) | copy-start | bytes 22020100
  163.9 13.3 %copy-start.2 = (bf16[512,896]{1,0:T(8,128)(2,1)S(1)}, bf16[512,896]{1,0:T(8,128)(2,1)}, u32[]{:S(2)}) copy-start(bf16[512,896]{1,0:T(8,128)(2,1)} %get-tuple-element.12) | copy-start | bytes 2752516
  177.2 11.6 %copy-start = (bf16[128,896]{1,0:T(8,128)(2,1)S(1)}, bf16[128,896]{1,0:T(8,128)(2,1)}, u32[]{:S(2)}) copy-start(bf16[128,896]{1,0:T(8,128)(2,1)} %get-tuple-element.20) | copy-start | bytes 688132
Sparse Core Ops, SparseCore 0:
  164.0 24.6 reduce-scatter.1

commit v3 on v2

--- a/solution.py
+++ b/solution.py
@@ -45,13 +45,13 @@
     weight_in,
     weight_out,
     block_out,
-    token_part,
     active_out,
     hidden_out,
     features_out,
     upstream_out,
     *scratch,
 ):
+    token_parts, scratch = scratch[:n_row], scratch[n_row:]
     levels = n_col.bit_length() - 1
     piles = scratch[: levels]
     landed = scratch[levels : 2 * levels]
@@ -367,7 +367,11 @@
 
         @pl.when(t == steps - 1)
         def _():
-            token_part[...] = total[...].astype(BF)
+            for d in range(n_row):
+                goal = lax.rem(here + d, n_row)
+                token_parts[d][...] = total[
+                    pl.ds(pl.multiple_of(goal * rows, rows), rows), :
+                ].astype(BF)
 
     def written(t):
         @pl.when(t < chunks)
@@ -440,14 +444,14 @@
         functools.partial(kernel, n_row, n_col),
         out_shape=[
             shape((rows, depth), BF),
-            shape((tall, depth), BF),
             shape((tall, hidden), BF),
             shape((tall, hidden), BF),
             shape((tall, depth), BF),
             shape((tall, depth), BF),
-        ],
+        ]
+        + [shape((rows, depth), BF)] * n_row,
         in_specs=[vmem, vmem, anywhere, anywhere],
-        out_specs=[vmem, vmem, anywhere, anywhere, anywhere, anywhere],
+        out_specs=[vmem, anywhere, anywhere, anywhere, anywhere] + [vmem] * n_row,
         scratch_shapes=[pltpu.VMEM((2, tall >> j, width), BF) for j in range(levels)]
         + [pltpu.VMEM((RING, tall >> (j + 1), width), BF) for j in range(levels)]
         + [
@@ -482,12 +486,19 @@
 
 
 def shards(n_row, n_col, page_tokens, weight_in, weight_out, upstream):
-    block_out, token_part, active, grad_hidden, features, upstream_all = encode(
+    block_out, active, grad_hidden, features, upstream_all, *parts = encode(
         n_row, n_col, page_tokens, upstream, weight_in, weight_out
     )
-    grad_tokens = lax.psum_scatter(token_part, "row", scatter_dimension=0, tiled=True)
+    moved = [
+        lax.ppermute(parts[d], "row", [(i, (i + d) % n_row) for i in range(n_row)])
+        for d in range(n_row - 1, 0, -1)
+    ]
     grad_weight_in = contract_first(features, grad_hidden).astype(BF)
     grad_weight_out = contract_first(active, upstream_all).astype(BF)
+    total = parts[0].astype(F32)
+    for piece in moved:
+        total = total + piece.astype(F32)
+    grad_tokens = total.astype(BF)
     return (block_out, grad_tokens, grad_weight_in, grad_weight_out)
 
 

time: 196 us -> 185 us (0.944)
  between operations: 14.1 us -> 0.7 us
  starting transfers between devices: 0.04 us -> 3.16 us
    ppermute x0 -> x3, starting transfers between devices: none -> 3.16 us  [shards(): lax.ppermute(parts[d], 'row', [(i, (i + d) % n_row) for i in range(n_row)])]
  transfers between devices with their start and end apart: 1 -> 3, of which waited for: 1 -> 0; matrix products, arithmetic and copies ran while one was open for 12% -> 13% of each run, Pallas kernels for 0% -> 0%
where the time goes in v3:
time: 185 us
  Pallas kernels  157 us (85%)
  matrix products  23.2 us (13%)
  starting transfers between devices  3.16 us (2%)
    pallas_call x1, Pallas kernels, encode(): pl.pallas_call(functools.partial(kernel, n_row, n_col), out_shape=[shape(...  157 us
    dot_general x2, matrix products, contract_first(): lax.dot_general(left, right, (((0,), (0,)), ((), ())), preferred_element_...  23.2 us
  transfers between devices with their start and end apart: 3, of which 0 were waited for; matrix products, arithmetic and copies ran while one was open for 13% of the time, Pallas kernels for 0%

profile of v3, /device:TPU:0, one launch (start us, length us, event | category | flops | bytes accessed | tf_op | source)
XLA Modules:
  0.0 185.3 jit_solution(3379725846789125258)
XLA Ops:
  0.6 156.7 %shard_map.75 = (bf16[128,896]{1,0:T(8,128)(2,1)}, bf16[512,7168]{1,0:T(8,128)(2,1)}, bf16[512,7168]{1,0:T(8,128)(2,1)}, bf16[512,896]{1,0:T(8,128)(2,1)}, bf16[...) custom-call(bf16[128,896]{1,0:T(8,128)(2,1)} %tokens_ref.1, ...), custom_call_target="tpu_custom_call" | custom-call | flops 26306674688 | bytes 51380224 | tf_op jit(solution)/shard_map/pallas_call | solution.py:443
  157.4 0.0 slice-start
  157.4 0.0 copy-start.2
  157.4 2.5 %collective-permute-start = (bf16[128,896]{1,0:T(8,128)(2,1)}, bf16[128,896]{1,0:T(8,128)(2,1)S(1)}, u32[]{:S(2)}, u32[]{:S(2)}) collective-permute-start(bf16[128,896]{1,0:T(8,128)(2,1)} %get-tuple-element.15), channel_id=1, source_target_pairs={{0,24},{8,0},{16,8},{24,16},{1,25},{9,1},{17,9},{25,17},{2,26},{10... | collective-permute-start | bytes 688136 | tf_op jit(solution)/shard_map/ppermute | solution.py:493
  159.9 0.0 collective-permute-start.1
  159.9 0.6 collective-permute-start.2
  160.6 0.0 slice-start.1
  160.6 12.3 %convolution_convert_fusion.1 = bf16[896,7168]{1,0:T(8,128)(2,1)} fusion(bf16[512,896]{1,0:T(8,128)(2,1)} %get-tuple-element.18, bf16[512,7168]{1,0:T(8,128)(2,1)} %get-tuple-element.19), kind=kOutput, calls=%fused_computation.1 | convolution fusion | flops 6583091200 | bytes 21102592 | tf_op jit(solution)/shard_map/dot_general | solution.py:37
  172.8 0.0 slice-done
  172.8 0.0 copy-done.2
  172.8 0.0 slice-done.1
  172.9 0.0 copy-start.1
  172.9 0.0 copy-start
  172.9 10.9 %convolution_convert_fusion = bf16[7168,896]{1,0:T(8,128)(2,1)} fusion(bf16[512,7168]{1,0:T(8,128)(2,1)S(1)} %bitcast.5, bf16[512,896]{1,0:T(8,128)(2,1)S(1)} %copy-done.2), kind=kOutput, calls=%fused_computation | convolution fusion | flops 6583091200 | bytes 21102592 | tf_op jit(solution)/shard_map/dot_general | solution.py:37
  183.8 0.0 collective-permute-done
  183.8 0.0 collective-permute-done.1
  183.8 0.0 collective-permute-done.2
  183.8 0.0 copy-done.1
  183.8 0.8 add_convert_fusion
  184.6 0.0 copy-done
  184.6 0.7 copy.9
  (1 shorter events, 0.0 us)
Async XLA Ops:
  157.4 15.5 %slice-start = ((s8[7340032]{0:T(1024)(128)(4,1)}), s8[4194304]{0:T(1024)(128)(4,1)S(1)}, s32[]{:S(2)}) async-start(s8[7340032]{0:T(1024)(128)(4,1)} %bitcast.4), calls=%async_computation | async-start | bytes 8388608
  157.4 15.5 %copy-start.2 = (bf16[512,896]{1,0:T(8,128)(2,1)S(1)}, bf16[512,896]{1,0:T(8,128)(2,1)}, u32[]{:S(2)}) copy-start(bf16[512,896]{1,0:T(8,128)(2,1)} %get-tuple-element.21) | copy-start | bytes 2752516
  157.4 26.4 %collective-permute-start = (bf16[128,896]{1,0:T(8,128)(2,1)}, bf16[128,896]{1,0:T(8,128)(2,1)S(1)}, u32[]{:S(2)}, u32[]{:S(2)}) collective-permute-start(bf16[128,896]{1,0:T(8,128)(2,1)} %get-tuple-element.15), channel_id=1, source_target_pairs={{0,24},{8,0},{16,8},{24,16},{1,25},{9,1},{17,9},{25,17},{2,26},{10... | collective-permute-start | bytes 688136 | tf_op jit(solution)/shard_map/ppermute | solution.py:493
  159.9 23.9 %collective-permute-start.1 = (bf16[128,896]{1,0:T(8,128)(2,1)}, bf16[128,896]{1,0:T(8,128)(2,1)S(1)}, u32[]{:S(2)}, u32[]{:S(2)}) collective-permute-start(bf16[128,896]{1,0:T(8,128)(2,1)} %get-tuple-element.16), channel_id=1, source_target_pairs={{0,16},{8,24},{16,0},{24,8},{1,17},{9,25},{17,1},{25,9},{2,18},{10... | collective-permute-start | bytes 688136 | tf_op jit(solution)/shard_map/ppermute | solution.py:493
  159.9 23.9 %collective-permute-start.2 = (bf16[128,896]{1,0:T(8,128)(2,1)}, bf16[128,896]{1,0:T(8,128)(2,1)S(1)}, u32[]{:S(2)}, u32[]{:S(2)}) collective-permute-start(bf16[128,896]{1,0:T(8,128)(2,1)} %get-tuple-element.17), channel_id=1, source_target_pairs={{0,8},{8,16},{16,24},{24,0},{1,9},{9,17},{17,25},{25,1},{2,10},{10... | collective-permute-start | bytes 688136 | tf_op jit(solution)/shard_map/ppermute | solution.py:493
  160.6 12.3 %slice-start.1 = ((s8[7340032]{0:T(1024)(128)(4,1)}), s8[3145728]{0:T(1024)(128)(4,1)S(1)}, s32[]{:S(2)}) async-start(s8[7340032]{0:T(1024)(128)(4,1)} %bitcast.4), calls=%async_computation.1 | async-start | bytes 6291456
  172.9 10.9 %copy-start.1 = (bf16[128,896]{1,0:T(8,128)(2,1)S(1)}, bf16[128,896]{1,0:T(8,128)(2,1)}, u32[]{:S(2)}) copy-start(bf16[128,896]{1,0:T(8,128)(2,1)} %get-tuple-element.14) | copy-start | bytes 688132
  172.9 11.7 %copy-start = (bf16[128,896]{1,0:T(8,128)(2,1)S(1)}, bf16[128,896]{1,0:T(8,128)(2,1)}, u32[]{:S(2)}) copy-start(bf16[128,896]{1,0:T(8,128)(2,1)} %get-tuple-element.26) | copy-start | bytes 688132
